TPU v7x, 32 devices: a whole 2x2x4 slice. The times are simulated.
32 devices in a mesh: ctx: 8 (over z, y), head: 4 (over x, core).
Axes of the slice: x: 2, y: 2, z: 4, core: 2. Of those that a mesh axis runs over, the one named last changes fastest.
Arguments:
- features: bfloat16 [8192, 16384], P('ctx', 'head'), may hold values from -6 to 6
- gates: bfloat16 [8192, 16384], P('ctx', 'head'), may hold values from -6 to 6
- state_io: bfloat16 [8192, 2, 2048], P('ctx', None, 'head'), may hold values from -6 to 6
- step_size: float32 [256, 8192], P('head', 'ctx'), may hold values from 0.004 to 0.02
- log_decay: float32 [256, 8192], P('head', 'ctx'), may hold values from -2 to 0, as said below
- conv_feat: bfloat16 [4, 16384], P(None, 'head'), may hold values from -3 to 3
- conv_state: bfloat16 [4, 2, 2048], P(None, None, 'head'), may hold values from -3 to 3
- skip_gain: float32 [256], P('head'), may hold values from 0.5 to 1.5
- norm_gain: float32 [16384], P('head'), may hold values from 0.25 to 1.75
Outputs:
- mixed: bfloat16 [8192, 16384], P(('ctx', 'head'))
Inputs may be any that keep to these rules, and one draw needn't show every extreme that they name: `log_decay`: every entry is negative.
All inputs are finite; a program needn't handle non-finite values.
Results may differ from a plain program's by a relative error of at most 0.0034.
Values may be sent and summed in bfloat16 or wider, within the bound.
No kernel may reach another device: no remote copies, remote signals or barrier semaphores. Data moves between devices by JAX's collectives and lax.ppermute only.
A program may use at most 256 MiB of HBM per device.

v0:
```python
import jax
import jax.numpy as jnp
from jax import lax
from jax.sharding import PartitionSpec as P

STATE = 256
SPAN = 128


def passed_along(value, axis, steps):
    count = lax.axis_size(axis)
    initial, last = (max(0, -steps), min(count, count - steps))
    return lax.ppermute(value, axis, [(source, source + steps) for source in range(initial, last)])


def conv_rows(padded, kernel, length):
    taps = kernel.shape[0]
    summed = jnp.zeros((length,) + padded.shape[1:], jnp.float32)
    for offset in range(taps):
        summed = summed + kernel[offset].astype(jnp.float32) * padded[
            offset : offset + length
        ].astype(jnp.float32)
    return jax.nn.silu(summed).astype(jnp.bfloat16)


def shards(
    features, gates, state_io, step_size, log_decay, conv_feat, conv_state, skip_gain, norm_gain
):
    tok_rows = features.shape[0]
    inner_cols = features.shape[1]
    head_count = step_size.shape[0]
    head_dim = inner_cols // head_count
    state_cols = state_io.shape[2]
    group_count = state_cols // STATE
    per_group = head_count // group_count
    rim_rows = conv_feat.shape[0] - 1
    span_count = tok_rows // SPAN
    tail_rows = jnp.concatenate(
        [
            features[tok_rows - rim_rows :],
            state_io[tok_rows - rim_rows :].reshape(rim_rows, 2 * state_cols),
        ],
        axis=1,
    )
    before = passed_along(tail_rows, "ctx", 1)
    conv_out = conv_rows(
        jnp.concatenate([before[:, :inner_cols], features], axis=0), conv_feat, tok_rows
    )
    conv_io = conv_rows(
        jnp.concatenate(
            [before[:, inner_cols:].reshape(rim_rows, 2, state_cols), state_io], axis=0
        ),
        conv_state,
        tok_rows,
    )
    feat_spans = conv_out.reshape(span_count, SPAN, group_count, per_group, head_dim)
    io_spans = conv_io.reshape(span_count, SPAN, 2, group_count, STATE)
    in_maps = io_spans[:, :, 0]
    out_maps = io_spans[:, :, 1]
    step_spans = step_size.reshape(group_count, per_group, span_count, SPAN).transpose(2, 0, 1, 3)
    cumulated = jnp.cumsum(
        log_decay.reshape(group_count, per_group, span_count, SPAN).transpose(2, 0, 1, 3), axis=3
    )
    scores = jnp.einsum("ctgn,csgn->cgts", out_maps, in_maps, preferred_element_type=jnp.float32)
    lower_mask = jnp.tril(jnp.ones((SPAN, SPAN), dtype=bool))
    gaps = cumulated[..., :, None] - cumulated[..., None, :]
    weights = (
        scores[:, :, None]
        * jnp.exp(jnp.where(lower_mask, gaps, -jnp.inf))
        * step_spans[..., None, :]
    ).astype(jnp.bfloat16)
    output_diag = jnp.einsum(
        "cgjts,csgjp->ctgjp", weights, feat_spans, preferred_element_type=jnp.float32
    )
    span_end = cumulated[..., -1:]
    weighting = jnp.exp(span_end - cumulated) * step_spans
    scaled_in = (
        weighting.transpose(0, 3, 1, 2)[..., None] * feat_spans.astype(jnp.float32)
    ).astype(jnp.bfloat16)
    local_state = jnp.einsum(
        "csgjp,csgn->cgjpn", scaled_in, in_maps, preferred_element_type=jnp.float32
    )
    span_log = span_end[..., 0]

    def advance(carried, pieces):
        log_total, added = pieces
        return (jnp.exp(log_total)[..., None, None] * carried + added, carried)

    zero_state = jnp.zeros(local_state.shape[1:], jnp.float32)
    dev_state, starts = lax.scan(advance, zero_state, (span_log, local_state))
    dev_decay = jnp.exp(jnp.sum(span_log, axis=0))
    start_log = jnp.cumsum(span_log, axis=0) - span_log
    all_decay, all_state = (
        lax.all_gather(dev_decay[None], "ctx", axis=0, tiled=True),
        lax.all_gather(dev_state[None], "ctx", axis=0, tiled=True),
    )
    my_rank = lax.axis_index("ctx")

    def absorb(carried, pieces):
        source_rank, decay_one, state_one = pieces
        return (
            jnp.where(
                source_rank < my_rank, decay_one[..., None, None] * carried + state_one, carried
            ),
            None,
        )

    ranks = jnp.arange(all_decay.shape[0], dtype=jnp.int32)
    incoming, _ = lax.scan(absorb, jnp.zeros_like(dev_state), (ranks, all_decay, all_state))
    span_state = jnp.exp(start_log)[..., None, None] * incoming[None] + starts
    state_low = span_state.astype(jnp.bfloat16)
    output_carried = (
        jnp.einsum("ctgn,cgjpn->ctgjp", out_maps, state_low, preferred_element_type=jnp.float32)
        * jnp.exp(cumulated).transpose(0, 3, 1, 2)[..., None]
    )
    skip_rows = skip_gain.reshape(group_count, per_group)[None, None, :, :, None]
    mixed_in = output_diag + output_carried + skip_rows * feat_spans.astype(jnp.float32)
    gated_out = mixed_in * jax.nn.silu(
        gates.reshape(span_count, SPAN, group_count, per_group, head_dim).astype(jnp.float32)
    )
    mean_square = jnp.mean(gated_out * gated_out, axis=(3, 4), keepdims=True)
    normed = (
        gated_out
        * lax.rsqrt(mean_square + 1e-05)
        * norm_gain.reshape(group_count, per_group, head_dim)
    ).astype(jnp.bfloat16)
    normed = normed.reshape(tok_rows, inner_cols)
    return lax.all_to_all(normed, "head", split_axis=0, concat_axis=1, tiled=True)


def solution(mesh):
    in_specs = (
        P("ctx", "head"),
        P("ctx", "head"),
        P("ctx", None, "head"),
        P("head", "ctx"),
        P("head", "ctx"),
        P(None, "head"),
        P(None, None, "head"),
        P("head"),
        P("head"),
    )
    out_specs = P(("ctx", "head"), None)
    return jax.shard_map(shards, mesh=mesh, in_specs=in_specs, out_specs=out_specs, check_vma=False)
```

profile of v0, /device:TPU:0, one launch (start us, length us, event | category | flops | bytes accessed | tf_op | source)
XLA Modules:
  0.0 1110.0 jit_solution(14238984561433061934)
XLA Ops:
  8.1 4.9 collective-permute-start
  15.1 4.6 reduce_window_sum.24
  23.4 18.7 %multiply_convert_fusion.3 = bf16[1024,4096]{1,0:T(8,128)(2,1)} fusion(bf16[1024,4096]{1,0:T(8,128)(2,1)} %param.13, bf16[3,4096]{1,0:T(4,128)(2,1)S(1)} %slice.84, f32[4096]{0:T(1024)S(1)} %bitcast.114, f32[4096]{0:T(1024)S(1)} %bitcast.115, f32[4096]{0:T(1024)S(1)} %bitcast.113, f32[4096]{0:T(1024)S(1)} %bitcast.112), kind=kLoop, calls=%fused_computation.26 | loop fusion | flops 104857600 | bytes 16867328 | tf_op jit(solution)/shard_map/convert_element_type | solution.py:23
  42.1 23.6 %reshape.95 = bf16[8,128,2,32,64]{4,3,2,1,0:T(8,128)(2,1)} reshape(bf16[1024,4096]{1,0:T(8,128)(2,1)} %multiply_convert_fusion.3) | data formatting | bytes 16777216 | tf_op jit(solution)/shard_map/reshape | solution.py:56
  65.7 21.7 %copy.53 = bf16[8,128,2,32,64]{1,4,3,2,0:T(8,128)(2,1)} copy(bf16[8,128,2,32,64]{4,3,2,1,0:T(8,128)(2,1)} %reshape.95) | data formatting | bytes 16777216 | tf_op jit(solution)/shard_map/reshape | solution.py:56
  87.4 1.6 constant_dynamic-update-slice_fusion
  89.0 10.4 fusion.20
  99.4 6.0 reshape.94
  105.4 2.3 fusion.31
  107.7 15.4 %fusion.17 = f32[8,2,32,64,256]{4,3,2,1,0:T(8,128)} fusion(bf16[8,128,2,32,64]{1,4,3,2,0:T(8,128)(2,1)} %copy.53, f32[8,128,2,32]{1,3,2,0:T(8,128)} %bitcast_multiply_fusion.1, bf16[8,128,1,2,256]{4,3,2,1,0:T(2,128)(2,1)S(1)} %get-tuple-element.145), kind=kOutput, calls=%fused_computation.32 | convolution fusion | flops 2160066560 | bytes 43253760 | tf_op jit(solution)/shard_map/csgjp,csgn->cgjpn/dot_general | solution.py:80
  123.1 82.3 %while.24 = (s32[]{:T(128)}, f32[2,32,64,256]{3,2,1,0:T(8,128)}, f32[8,2,32,64,256]{4,3,2,1,0:T(8,128)}, f32[8,2,32]{2,1,0:T(2,128)S(1)}, f32[8,2,32,64,256]{4,3,2,1,0:T(8,128)}, /*index=5*/s32[]{:T(128)}, s32[]{:T(128)}) while((s32[]{:T(128)}, f32[2,32,64,256]{3,2,1,0:T(8,128)}, f32[8,2,32,64,256]{4,3,2,1,0:T(8,128)}, ...), condition=%wide.region_4.5_spmd.clone, body=%wide.region_3.4_spmd.clone.sunk | while | flops 4194307 | bytes 20972896 | solution.py:90
  123.1 2.6 bitcast_dynamic-update-slice_fusion.2
  125.7 4.7 bitcast_add_fusion.3
  130.5 4.7 bitcast_dynamic-update-slice_fusion.2
  135.2 6.0 bitcast_add_fusion.3
  141.2 4.7 bitcast_dynamic-update-slice_fusion.2
  145.9 6.0 bitcast_add_fusion.3
  151.9 4.7 bitcast_dynamic-update-slice_fusion.2
  156.5 6.0 bitcast_add_fusion.3
  162.5 4.8 bitcast_dynamic-update-slice_fusion.2
  167.3 6.0 bitcast_add_fusion.3
  173.3 4.7 bitcast_dynamic-update-slice_fusion.2
  178.0 6.0 bitcast_add_fusion.3
  184.0 4.7 bitcast_dynamic-update-slice_fusion.2
  188.7 6.0 bitcast_add_fusion.3
  194.7 4.7 bitcast_dynamic-update-slice_fusion.2
  199.4 6.0 bitcast_add_fusion.3
  206.3 24.0 %reshape.96 = f32[8,128,2,32,64]{4,3,2,1,0:T(8,128)} reshape(bf16[1024,4096]{1,0:T(8,128)(2,1)} %param.14) | data formatting | bytes 25165824 | tf_op jit(solution)/shard_map/convert_element_type | solution.py:119
  230.3 27.5 %copy.62 = f32[8,128,2,32,64]{1,4,3,2,0:T(8,128)} copy(f32[8,128,2,32,64]{4,3,2,1,0:T(8,128)} %reshape.96) | data formatting | bytes 33554432 | tf_op jit(solution)/shard_map/convert_element_type | solution.py:119
  258.0 18.8 %all-gather.2 = f32[8,2,32]{2,1,0:T(2,128)S(1)} all-gather(f32[1,2,32]{2,1,0:T(2,128)S(1)} %exponential_bitcast_fusion.2), channel_id=2, replica_groups=mesh['ctx'=8,'head'=4] {'ctx'}, dimensions={0}, use_global_device_ids=true | all-gather | bytes 2304 | tf_op jit(solution)/shard_map/all_gather | solution.py:94
  278.0 15.7 %fusion.1 = f32[8,2,32,64,128]{4,3,2,1,0:T(8,128)} fusion(bf16[8,128,2,32,64]{1,4,3,2,0:T(8,128)(2,1)} %copy.53, f32[8,2,32,128]{3,2,1,0:T(8,128)} %copy.52, f32[8,2,32,128]{3,2,1,0:T(8,128)S(1)} %reduce_window_sum.24, f32[8,2,128,128]{3,2,1,0:T(8,128)S(1)} %fusion.23, pred[128,128]{1,0:T(8,128)(4,1)S(1)} %iota_compare_fusion), kind=kOutput, calls=%fused_computation.10 | convolution fusion | flops 1115684864 | bytes 26755072 | tf_op jit(solution)/shard_map/cgjts,csgjp->ctgjp/dot_general | solution.py:72
  293.7 550.1 %all-gather.5.cloned.1.call-done = f32[16,32,64,256]{3,2,1,0:T(8,128)} async-done(((f32[2,32,64,256]{3,2,1,0:T(8,128)}), f32[16,32,64,256]{3,2,1,0:T(8,128)}) %all-gather.5.cloned.1.call-update) | async-done | bytes 33554448 | tf_op jit(solution)/shard_map/all_gather | solution.py:95
  843.8 58.0 %while.25 = (s32[]{:T(128)}, f32[2,32,64,256]{3,2,1,0:T(8,128)}, s32[8]{0:T(128)S(1)}, s32[]{:T(128)}, f32[8,2,32]{2,1,0:T(2,128)S(1)}, /*index=5*/f32[8,2,32,64,256]{4,3,2,1,0:T(8,128)}, s32[]{:T(128)}, s32[]{:T(128)}) while((s32[]{:T(128)}, f32[2,32,64,256]{3,2,1,0:T(8,128)}, s32[8]{0:T(128)S(1)}, s32[]{:T(128)}, ...), condition=%wide.region_6.7_spmd.clone, body=%wide.region_5.6_spmd.clone.sunk | while | flops 4194308 | bytes 12583805 | solution.py:109
  845.2 4.7 fusion.34
  851.3 6.0 fusion.34
  858.7 6.0 fusion.34
  866.1 6.0 fusion.34
  873.6 6.0 fusion.34
  881.0 6.0 fusion.34
  888.4 6.0 fusion.34
  895.8 6.0 fusion.34
  901.8 32.9 %multiply_reduce_fusion = (f32[8,128,2]{1,2,0:T(2,128)S(1)}, f32[8,128,2,32,64]{1,4,3,2,0:T(8,128)}) fusion(f32[8,128,2,32,64]{1,4,3,2,0:T(8,128)} %copy.62, bf16[8,128,2,32,64]{1,4,3,2,0:T(8,128)(2,1)} %copy.53, f32[2,32]{1,0:T(2,128)S(1)} %mul.263, f32[8,128,2,32]{1,3,2,0:T(8,128)S(1)} %copy-done.4, bf16[8,128,1,2,256]{4,3,2,1,0:T(2,128)(2,1)S(1)} %copy-done.1, ...), kind=kOutput, calls=%fused_computation.18 | convolution fusion | flops 2222979072 | bytes 97790208 | tf_op jit(solution)/shard_map/ctgn,cgjpn->ctgjp/dot_general | solution.py:113
  934.8 10.1 multiply_convert_fusion.2
  944.9 23.6 %copy.63 = bf16[8,128,2,32,64]{1,0,4,3,2:T(8,128)(2,1)} copy(bf16[8,128,2,32,64]{1,4,3,2,0:T(8,128)(2,1)} %multiply_convert_fusion.2) | data formatting | bytes 16777216 | tf_op jit(solution)/shard_map/convert_element_type | solution.py:126
  968.5 14.0 %all_to_all.14 = bf16[4,256,4096]{1,0,2:T(4,128)(2,1)} reshape(bf16[8,128,2,32,64]{1,0,4,3,2:T(8,128)(2,1)} %copy.63) | data formatting | bytes 16777216 | tf_op jit(solution)/shard_map/all_to_all | solution.py:128
  982.5 7.7 copy.64
  990.2 100.6 %all_to_all.19 = bf16[4,256,4096]{1,2,0:T(8,128)(2,1)} all-to-all(bf16[4,256,4096]{1,2,0:T(8,128)(2,1)} %copy.64), channel_id=1, replica_groups=mesh['ctx'=8,'head'=4] {'head'}, dimensions={0} | all-to-all | bytes 16777216 | tf_op jit(solution)/shard_map/all_to_all | solution.py:128
  1090.8 11.9 %copy.65 = bf16[256,16384]{1,0:T(8,128)(2,1)} copy(bf16[256,16384]{0,1:T(8,128)(2,1)} %bitcast.102) | data formatting | bytes 16777216 | tf_op jit(solution)/shard_map/all_to_all | solution.py:128
  (74 shorter events, 15.0 us)
Async XLA Ops:
  6.5 837.3 %all-gather.5.cloned.1.call-start = ((), (), s32[]{:S(2)}) async-start(), calls=%async_computation.1 | async-start | bytes 37748736 | tf_op jit(solution)/shard_map/all_gather | solution.py:95
  8.1 15.3 %collective-permute-start = (bf16[3,5120]{1,0:T(4,128)(2,1)S(1)}, bf16[3,5120]{1,0:T(4,128)(2,1)S(1)}, u32[]{:S(2)}, u32[]{:S(2)}) collective-permute-start(bf16[3,5120]{1,0:T(4,128)(2,1)S(1)} %pad_maximum_fusion.1), channel_id=1, source_target_pairs={{0,4},{4,8},{8,12},{12,16},{16,20},{20,24},{24,28},{1,5},{5,9},{9,... | collective-permute-start | bytes 92168 | tf_op jit(solution)/shard_map/ppermute | solution.py:13
  21.1 0.7 copy-start.2
  65.7 21.7 %copy-start = (bf16[1024,2,512]{2,1,0:T(2,128)(2,1)S(1)}, bf16[1024,2,512]{2,1,0:T(2,128)(2,1)}, u32[]{:S(2)}) copy-start(bf16[1024,2,512]{2,1,0:T(2,128)(2,1)} %param.15) | copy-start | bytes 6291460
  123.1 82.4 %copy-start.3 = (f32[8,8,8,128]{3,2,1,0:T(8,128)S(1)}, f32[8,8,8,128]{3,2,1,0:T(8,128)}, u32[]{:S(2)}) copy-start(f32[8,8,8,128]{3,2,1,0:T(8,128)} %copy-done.2) | copy-start | bytes 786436
  230.3 27.6 %copy-start.6 = (f32[64]{0:T(128)S(1)}, f32[64]{0:T(128)}, u32[]{:S(2)}) copy-start(f32[64]{0:T(128)} %param.20) | copy-start | bytes 772
  230.3 27.6 %copy-start.5 = (f32[4096]{0:T(1024)S(1)}, f32[4096]{0:T(1024)}, u32[]{:S(2)}) copy-start(f32[4096]{0:T(1024)} %param.21) | copy-start | bytes 49156
  230.3 47.2 %copy-start.1 = (bf16[8,128,1,2,256]{4,3,2,1,0:T(2,128)(2,1)S(1)}, bf16[8,128,1,2,256]{4,3,2,1,0:T(2,128)(2,1)}, u32[]{:S(2)}) copy-start(bf16[8,128,1,2,256]{4,3,2,1,0:T(2,128)(2,1)} %get-tuple-element.144) | copy-start | bytes 3145732
  843.8 58.0 %copy-start.4 = (f32[8,128,2,32]{1,3,2,0:T(8,128)S(1)}, f32[8,128,2,32]{1,3,2,0:T(8,128)}, u32[]{:S(2)}) copy-start(f32[8,128,2,32]{1,3,2,0:T(8,128)} %exponential_bitcast_fusion.1) | copy-start | bytes 786436
Sparse Core Ops, SparseCore 0:
  205.6 638.1 all-gather.4
where the time goes:
time: 1120 us; the launch traced here: 1110 us
  waiting for transfers between devices  550 us (49%)
  local copies, waits for them, and re-layouts  176 us (16%)
  other arithmetic  176 us (16%)
  blocking collectives  119 us (11%)
  matrix products  64.4 us (6%)
  between operations  14 us (1%)
    all_gather x1, waiting for transfers between devices, shards(): lax.all_gather(dev_state[None], 'ctx', axis=0, tiled=True)  550 us
    all_to_all x1, blocking collectives, shards(): lax.all_to_all(normed, 'head', split_axis=0, concat_axis=1, tiled=True)  101 us
    convert_element_type x2, local copies, waits for them, and re-layouts, shards(): gates.reshape(span_count, SPAN, group_count, per_group, head_dim)  51.5 us
    select_n x8, other arithmetic, absorb(): jnp.where(source_rank < my_rank, decay_one[..., None, None] * carried + s...  46.9 us
    add x8, other arithmetic, advance(): return (jnp.exp(log_total)[..., None, None] * carried + added, carried)  46.8 us
    reshape x2, local copies, waits for them, and re-layouts, shards(): conv_out.reshape(span_count, SPAN, group_count, per_group, head_dim)  45.3 us
    dynamic_update_slice x8, other arithmetic, shards(): dev_state, starts = lax.scan(advance, zero_state, (span_log, local_state))  35.4 us
    all_to_all x3, local copies, waits for them, and re-layouts, shards(): lax.all_to_all(normed, 'head', split_axis=0, concat_axis=1, tiled=True)  33.6 us
  transfers between devices with their start and end apart: 2, of which 1 were waited for; matrix products, arithmetic and copies ran while one was open for 7% of the time, Pallas kernels for 0%

commit v1 on v0

v1 whole, which is shorter than its diff:
```python
import functools

import jax
import jax.numpy as jnp
import numpy as np
from jax import lax
from jax.experimental import pallas as pl
from jax.experimental.pallas import tpu as pltpu
from jax.sharding import PartitionSpec as P

STATE = 256
SPAN = 128
HALO = 16
EPS = 1e-05
F32 = jnp.float32
BF16 = jnp.bfloat16
VMEM_BYTES = 48 * 1024 * 1024


def dot(a, b):
    return jnp.dot(a, b, preferred_element_type=F32)


def silu(v):
    half = 0.5 * v
    return half * jnp.tanh(half) + half


def params(limit=VMEM_BYTES):
    return pltpu.CompilerParams(vmem_limit_bytes=limit)


def shift_table(taps):
    table = np.zeros(((taps - 1) * SPAN, HALO + SPAN), np.float32)
    for k in range(1, taps):
        for t in range(SPAN):
            table[(k - 1) * SPAN + t, HALO + t - k] = 1.0
    return table


def spread_table(heads, head_dim):
    head = np.arange(2 * heads) % heads
    return (head[:, None] == (np.arange(heads * head_dim) // head_dim)[None, :]).astype(np.float32)


def decay_kernel(log_ref, step_ref, col_ref, row_ref, loc_ref, dev_ref, ecum_ref, edev_ref):
    heads, tokens = log_ref.shape
    spans = tokens // SPAN
    r = lax.broadcasted_iota(jnp.int32, (SPAN, SPAN), 0)
    c = lax.broadcasted_iota(jnp.int32, (SPAN, SPAN), 1)
    upper = (r <= c).astype(F32)
    cums = []
    for k in range(spans):
        cums.append(
            jnp.dot(
                log_ref[:, k * SPAN : (k + 1) * SPAN],
                upper,
                precision=lax.Precision.HIGHEST,
                preferred_element_type=F32,
            )
        )
    totals = [cum[:, SPAN - 1 :] for cum in cums]
    before = [jnp.zeros_like(totals[0])]
    for k in range(spans - 1):
        before.append(before[-1] + totals[k])
    after = [jnp.zeros_like(totals[0])]
    for k in range(spans - 1, 0, -1):
        after.insert(0, after[0] + totals[k])

    def put(ref, k, value):
        high = value.astype(BF16).astype(F32)
        both = jnp.concatenate([high, value - high], axis=0)
        ref[k * SPAN : (k + 1) * SPAN, :] = both.T.astype(BF16)

    for k in range(spans):
        cum = cums[k]
        step = step_ref[:, k * SPAN : (k + 1) * SPAN]
        col_ref[k * SPAN : (k + 1) * SPAN, :] = jnp.concatenate([cum, cum], axis=0).T
        row_ref[:, k * SPAN : (k + 1) * SPAN] = cum - jnp.log(step)
        to_end = totals[k] - cum
        put(loc_ref, k, jnp.exp(to_end) * step)
        put(dev_ref, k, jnp.exp(to_end + after[k]) * step)
        put(ecum_ref, k, jnp.exp(cum))
        put(edev_ref, k, jnp.exp(cum + before[k]))


def decay_tables(log_decay, step_size):
    heads, tokens = log_decay.shape
    wide = jax.ShapeDtypeStruct((tokens, 2 * heads), BF16)
    return pl.pallas_call(
        decay_kernel,
        out_shape=(
            jax.ShapeDtypeStruct((tokens, 2 * heads), F32),
            jax.ShapeDtypeStruct((heads, tokens), F32),
            wide,
            wide,
            wide,
            wide,
        ),
        compiler_params=params(),
        name="decays",
        cost_estimate=pl.CostEstimate(flops=10**8, bytes_accessed=3 * 10**6, transcendentals=4 * heads * tokens),
    )(log_decay, step_size)


def conv_rows(x_ref, halo, taps, shifts, store):
    rows = x_ref.shape[0]
    count = taps.shape[0]
    for b in range(rows // SPAN):
        own = x_ref[b * SPAN : (b + 1) * SPAN, :]
        prev = halo if b == 0 else x_ref[b * SPAN - HALO : b * SPAN, :]
        moved = dot(shifts, jnp.concatenate([prev, own], axis=0))
        total = own.astype(F32) * taps[count - 1 : count]
        for k in range(1, count):
            total = total + moved[(k - 1) * SPAN : k * SPAN] * taps[count - 1 - k : count - k]
        store(b, silu(total).astype(BF16))


def front_kernel(
    feat_ref, halo_ref, taps_ref, in_ref, in_halo_ref, in_taps_ref, out_ref, out_halo_ref, out_taps_ref,
    dev_ref, spread_ref, shift_ref, xh_ref, in_map_ref, out_map_ref, state_ref, in_turned, scaled,
):
    shifts = shift_ref[...]

    @pl.when(pl.program_id(0) == 0)
    def _():
        def put_in(b, value):
            in_map_ref[b * SPAN : (b + 1) * SPAN, :] = value
            in_turned[:, b * SPAN : (b + 1) * SPAN] = value.T

        def put_out(b, value):
            out_map_ref[b * SPAN : (b + 1) * SPAN, :] = value

        conv_rows(in_ref, in_halo_ref[...], in_taps_ref[...].astype(F32), shifts, put_in)
        conv_rows(out_ref, out_halo_ref[...], out_taps_ref[...].astype(F32), shifts, put_out)

    spread = spread_ref[...]

    def put_feat(b, value):
        rows = slice(b * SPAN, (b + 1) * SPAN)
        xh_ref[rows, :] = value
        scaled[rows, :] = (value.astype(F32) * dot(dev_ref[rows, :], spread)).astype(BF16)

    conv_rows(feat_ref, halo_ref[...], taps_ref[...].astype(F32), shifts, put_feat)
    state_ref[...] = dot(in_turned[...], scaled[...])


def front(group, width, features, halo, conv_feat, maps, map_halos, map_taps, dev_table, spread, shifts):
    tokens = features.shape[0]
    block = min(512, width)
    steps = width // block
    count = conv_feat.shape[0]
    heads2 = dev_table.shape[1]

    def cols(j):
        return (0, group * steps + j)

    def mine(j):
        return (0, group)

    def same(j):
        return (0, 0)

    map_specs = [
        pl.BlockSpec((tokens, STATE), mine),
        pl.BlockSpec((HALO, STATE), mine),
        pl.BlockSpec((count, STATE), mine),
    ]
    return pl.pallas_call(
        front_kernel,
        grid=(steps,),
        in_specs=[
            pl.BlockSpec((tokens, block), cols),
            pl.BlockSpec((HALO, block), cols),
            pl.BlockSpec((count, block), cols),
            *map_specs,
            *map_specs,
            pl.BlockSpec((tokens, heads2), same),
            pl.BlockSpec((heads2, block), cols),
            pl.BlockSpec(shifts.shape, same),
        ],
        out_specs=[
            pl.BlockSpec((tokens, block), lambda j: (0, j)),
            pl.BlockSpec((tokens, STATE), same),
            pl.BlockSpec((tokens, STATE), same),
            pl.BlockSpec((STATE, block), lambda j: (0, j)),
        ],
        out_shape=(
            jax.ShapeDtypeStruct((tokens, width), BF16),
            jax.ShapeDtypeStruct((tokens, STATE), BF16),
            jax.ShapeDtypeStruct((tokens, STATE), BF16),
            jax.ShapeDtypeStruct((STATE, width), F32),
        ),
        scratch_shapes=[pltpu.VMEM((STATE, tokens), BF16), pltpu.VMEM((tokens, block), BF16)],
        compiler_params=params(),
        name=f"front{group}",
        cost_estimate=pl.CostEstimate(
            flops=8 * 10**9, bytes_accessed=tokens * width * 4, transcendentals=tokens * width
        ),
    )(
        features, halo, conv_feat, maps[0], map_halos[0], map_taps[0], maps[1], map_halos[1], map_taps[1],
        dev_table, spread, shifts,
    )


def span_kernel(
    first_head, xh_ref, in_ref, out_ref, col_ref, row_ref, loc_ref, ecum_ref, spread_ref, skip_ref, halves_ref,
    y_ref, state, scaled,
):
    width = xh_ref.shape[1]
    per_group = row_ref.shape[0]
    head_dim = width // per_group

    @pl.when(pl.program_id(0) == 0)
    def _():
        state[...] = jnp.zeros_like(state)

    in_map = in_ref[...]
    out_map = out_ref[...]
    scores = lax.dot_general(out_map, in_map, (((1,), (1,)), ((), ())), preferred_element_type=F32)
    t = lax.broadcasted_iota(jnp.int32, (SPAN, SPAN), 0)
    s = lax.broadcasted_iota(jnp.int32, (SPAN, SPAN), 1)
    scores = jnp.where(s <= t, scores, 0.0)
    in_turned = in_map.T
    first = halves_ref[0:1, :]
    second = halves_ref[1:2, :]
    block = 256
    for q in range(width // block):
        cols = slice(q * block, (q + 1) * block)
        spread = spread_ref[:, cols]
        feats = xh_ref[:, cols]
        feats32 = feats.astype(F32)
        scaled[:, cols] = (feats32 * dot(loc_ref[...], spread)).astype(BF16)
        ecum = dot(ecum_ref[...], spread)
        pairs = []
        for p in range(block // 128):
            weights = []
            for i in range(2):
                h = (q * block + p * 128) // head_dim + i
                gap = col_ref[:, first_head + h : first_head + h + 1] - row_ref[h : h + 1, :]
                weights.append((scores * jnp.exp(jnp.minimum(gap, 0.0))).astype(BF16))
            pair = feats[:, p * 128 : (p + 1) * 128]
            stacked = jnp.concatenate([pair * first, pair * second], axis=0)
            pairs.append(dot(jnp.concatenate(weights, axis=1), stacked))
        diag = jnp.concatenate(pairs, axis=1)
        held = state[:, cols]
        carried = dot(out_map, held.astype(BF16)) * ecum
        y_ref[:, cols] = diag + carried + skip_ref[:, cols] * feats32
        state[:, cols] = ecum[SPAN - 1 :] * held + dot(in_turned, scaled[:, cols])


def spans_of(group, per_group, xh, in_map, out_map, col, row, loc, ecum, spread, skip_row, halves):
    tokens, width = xh.shape
    heads2 = loc.shape[1]
    return pl.pallas_call(
        functools.partial(span_kernel, group * per_group),
        grid=(tokens // SPAN,),
        in_specs=[
            pl.BlockSpec((SPAN, width), lambda k: (k, 0)),
            pl.BlockSpec((SPAN, STATE), lambda k: (k, 0)),
            pl.BlockSpec((SPAN, STATE), lambda k: (k, 0)),
            pl.BlockSpec((SPAN, heads2), lambda k: (k, 0)),
            pl.BlockSpec((per_group, SPAN), lambda k: (group, k)),
            pl.BlockSpec((SPAN, heads2), lambda k: (k, 0)),
            pl.BlockSpec((SPAN, heads2), lambda k: (k, 0)),
            pl.BlockSpec((heads2, width), lambda k: (0, group)),
            pl.BlockSpec((1, width), lambda k: (0, group)),
            pl.BlockSpec(halves.shape, lambda k: (0, 0)),
        ],
        out_specs=pl.BlockSpec((SPAN, width), lambda k: (k, 0)),
        out_shape=jax.ShapeDtypeStruct((tokens, width), F32),
        scratch_shapes=[pltpu.VMEM((STATE, width), F32), pltpu.VMEM((SPAN, width), BF16)],
        compiler_params=params(),
        name=f"spans{group}",
        cost_estimate=pl.CostEstimate(
            flops=8 * 10**9, bytes_accessed=tokens * width * 6, transcendentals=tokens * per_group * SPAN
        ),
    )(xh, in_map, out_map, col, row, loc, ecum, spread, skip_row, halves)


def back_kernel(
    blk_ref, y_ref, out_ref, edev_ref, spread_ref, low_ref, high_ref, gate_ref, gain_ref, o_ref, gated
):
    rows, width = y_ref.shape
    out_map = out_ref[...]
    edev = edev_ref[...]
    block = 256
    half = low_ref.shape[1]
    squares = jnp.zeros((rows, block), F32)
    for q in range(width // block):
        cols = slice(q * block, (q + 1) * block)
        if q * block < half:
            state = low_ref[:, cols]
        else:
            state = high_ref[:, q * block - half : (q + 1) * block - half]
        carried = dot(out_map, state) * dot(edev, spread_ref[:, cols])
        value = (y_ref[:, cols] + carried) * silu(gate_ref[:, cols].astype(F32))
        squares = squares + value * value
        gated[:, cols] = value
    mean = jnp.sum(squares, axis=1, keepdims=True) * (1.0 / width)
    scale = lax.rsqrt(mean + EPS)
    for q in range(width // block):
        cols = slice(q * block, (q + 1) * block)
        o_ref[:, cols] = (gated[:, cols] * scale * gain_ref[:, cols]).astype(BF16)


def back(group, blk, rows, y, out_map, edev, spread, low, high, gates, gain_row):
    width = y.shape[1]
    heads2 = edev.shape[1]
    tile = 128
    steps = rows // tile

    def at(i, blk):
        return (blk[0] * steps + i, 0)

    grid_spec = pltpu.PrefetchScalarGridSpec(
        num_scalar_prefetch=1,
        grid=(steps,),
        in_specs=[
            pl.BlockSpec((tile, width), at),
            pl.BlockSpec((tile, STATE), at),
            pl.BlockSpec((tile, heads2), at),
            pl.BlockSpec((heads2, width), lambda i, blk: (0, group)),
            pl.BlockSpec((STATE, low.shape[1]), lambda i, blk: (0, 0)),
            pl.BlockSpec((STATE, high.shape[1]), lambda i, blk: (0, 0)),
            pl.BlockSpec((tile, width), lambda i, blk: (blk[0] * steps + i, group)),
            pl.BlockSpec((1, width), lambda i, blk: (0, group)),
        ],
        out_specs=pl.BlockSpec((tile, width), lambda i, blk: (i, 0)),
        scratch_shapes=[pltpu.VMEM((tile, width), F32)],
    )
    return pl.pallas_call(
        back_kernel,
        grid_spec=grid_spec,
        out_shape=jax.ShapeDtypeStruct((rows, width), BF16),
        compiler_params=params(),
        name=f"back{group}",
        cost_estimate=pl.CostEstimate(
            flops=10**9, bytes_accessed=rows * width * 8 + 3 * STATE * width, transcendentals=rows * width
        ),
    )(blk, y, out_map, edev, spread, low, high, gates, gain_row)


def shifted(value, pairs, steps):
    return lax.ppermute(
        value,
        "ctx",
        [(2 * q + y, 2 * (q + steps) + y) for q in range(pairs - steps) for y in range(2)],
    )


def swapped(value, pairs):
    return lax.ppermute(value, "ctx", [(2 * q + y, 2 * q + 1 - y) for q in range(pairs) for y in range(2)])


def incoming(state, own_decay, pair_decay, odd, pairs):
    half = state.shape[1] // 2
    halves = (state[:, :half], state[:, half:])
    keep = jnp.where(odd, halves[1], halves[0])
    got = swapped(jnp.where(odd, halves[0], halves[1]).astype(BF16), pairs).astype(F32)
    keep_own = own_decay
    keep_partner, keep_before = pair_decay
    even_state = jnp.where(odd, got, keep)
    total = jnp.where(odd, keep_own * got + keep, keep_partner * keep + got)
    total_decay = keep_own * keep_partner
    carried = shifted(total.astype(BF16), pairs, 1).astype(F32)
    decay = keep_before
    reach = 1
    while reach < pairs - 1:
        inclusive = total + total_decay * carried
        far = shifted(inclusive.astype(BF16), pairs, reach + 1).astype(F32)
        far_decay = shifted(total_decay * decay, pairs, reach + 1)
        carried = carried + decay * far
        decay = decay * far_decay
        reach = 2 * reach + 1
    return carried, even_state


def shards(
    features, gates, state_io, step_size, log_decay, conv_feat, conv_state, skip_gain, norm_gain
):
    tokens, channels = features.shape
    heads = step_size.shape[0]
    head_dim = channels // heads
    map_cols = state_io.shape[2]
    groups = map_cols // STATE
    per_group = heads // groups
    width = channels // groups
    half = width // 2
    count = conv_feat.shape[0]
    rim = count - 1
    ctx_size = lax.axis_size("ctx")
    head_size = lax.axis_size("head")
    pairs = ctx_size // 2
    rows = tokens // head_size
    me = lax.axis_index("head")
    odd = lax.axis_index("ctx") % 2 == 1

    tail = jnp.concatenate(
        [features[tokens - rim :], state_io[tokens - rim :, 0], state_io[tokens - rim :, 1]], axis=1
    )
    before = lax.ppermute(tail, "ctx", [(i, i + 1) for i in range(ctx_size - 1)])
    maps = (state_io[:, 0], state_io[:, 1])
    map_taps = (conv_state[:, 0], conv_state[:, 1])
    spread = jnp.asarray(spread_table(heads, head_dim), BF16)
    shifts = jnp.asarray(shift_table(count), BF16)
    halves = jnp.asarray(np.arange(128)[None, :] // head_dim == np.arange(2)[:, None], BF16)
    col, row, loc, dev, ecum, edev = decay_tables(log_decay, step_size)
    skip_row = jnp.repeat(skip_gain, head_dim)[None]
    gain_row = norm_gain[None]

    own_decay = jnp.repeat(jnp.exp(jnp.sum(log_decay, axis=1)), head_dim)[None]
    kept = [slice(g * width, g * width + half) for g in range(groups)]
    rest = [slice(g * width + half, (g + 1) * width) for g in range(groups)]
    partner_decay = swapped(own_decay, pairs)
    before_decay = shifted(own_decay * partner_decay, pairs, 1)

    def kept_half(value, g):
        return jnp.where(odd, value[:, rest[g]], value[:, kept[g]])

    before = jnp.pad(before, ((HALO - rim, 0), (0, 0)))
    halo = before[:, :channels]
    map_halos = (before[:, channels : channels + map_cols], before[:, channels + map_cols :])

    fronts = [
        front(g, width, features, halo, conv_feat, maps, map_halos, map_taps, dev, spread, shifts)
        for g in range(groups)
    ]
    states = []
    for g in range(groups):
        state = fronts[g][3]
        carried, even_state = incoming(
            state,
            kept_half(own_decay, g),
            (kept_half(partner_decay, g), kept_half(before_decay, g)),
            odd,
            pairs,
        )
        through = kept_half(own_decay, g) * carried + even_state
        mine = jnp.where(odd, kept_half(partner_decay, g) * carried + even_state, carried)
        other = swapped(jnp.where(odd, carried, through).astype(BF16), pairs)
        mine = mine.astype(BF16)
        states.append((jnp.where(odd, other, mine), jnp.where(odd, mine, other)))
    locals_ = [
        spans_of(
            g, per_group, fronts[g][0], fronts[g][1], fronts[g][2], col, row, loc, ecum, spread, skip_row, halves
        )
        for g in range(groups)
    ]
    order = list(range(head_size - 1, -1, -1))
    out = jnp.zeros((rows, channels * head_size), BF16)
    pieces = []
    for cross in (True, False):
        for g in range(groups):
            for r in order:
                if (r >= 2) != cross:
                    continue
                blk = (me ^ r).astype(jnp.int32)
                made = back(
                    g, blk[None], rows, locals_[g], fronts[g][2], edev, spread, states[g][0], states[g][1],
                    gates, gain_row,
                )
                if r:
                    made = lax.ppermute(made, "head", [(i, i ^ r) for i in range(head_size)])
                pieces.append((made, blk * channels + g * width))
    for made, start in pieces:
        out = lax.dynamic_update_slice(out, made, (jnp.int32(0), start))
    return out


def solution(mesh):
    in_specs = (
        P("ctx", "head"),
        P("ctx", "head"),
        P("ctx", None, "head"),
        P("head", "ctx"),
        P("head", "ctx"),
        P(None, "head"),
        P(None, None, "head"),
        P("head"),
        P("head"),
    )
    out_specs = P(("ctx", "head"), None)
    return jax.shard_map(shards, mesh=mesh, in_specs=in_specs, out_specs=out_specs, check_vma=False)
```

time: 1120 us -> 244 us (0.22)
  the two profiles are of different devices: /device:TPU:0 before, /device:TPU:25 now
where the time goes in v1:
time: 244 us; the launch traced here: 243 us
  waiting for transfers between devices  90.1 us (37%)
  Pallas kernels  77.3 us (32%)
  local copies, waits for them, and re-layouts  31.5 us (13%)
  starting transfers between devices  23.2 us (10%)
  other arithmetic  20.1 us (8%)
    ppermute x6, waiting for transfers between devices, shards(): made = lax.ppermute(made, 'head', [(i, i ^ r) for i in range(head_size)])  60.5 us
    pallas_call x2, Pallas kernels, spans_of(): pl.pallas_call(functools.partial(span_kernel, group * per_group), grid=(t...  29 us
    pallas_call x8, Pallas kernels, back(): pl.pallas_call(back_kernel, grid_spec=grid_spec, out_shape=jax.ShapeDtype...  24.3 us
    ppermute x5, waiting for transfers between devices, shifted(): lax.ppermute(value, 'ctx', [(2 * q + y, 2 * (q + steps) + y) for q in ran...  23.8 us
    pallas_call x2, Pallas kernels, front(): pl.pallas_call(front_kernel, grid=(steps,), in_specs=[pl.BlockSpec((token...  22.7 us
    unnamed x54, local copies, waits for them, and re-layouts  12.9 us
    ppermute x6, starting transfers between devices, shards(): made = lax.ppermute(made, 'head', [(i, i ^ r) for i in range(head_size)])  9.17 us
    dynamic_update_slice x8, local copies, waits for them, and re-layouts, shards(): out = lax.dynamic_update_slice(out, made, (jnp.int32(0), start))  8.02 us
  transfers between devices with their start and end apart: 17, of which 6 were waited for; matrix products, arithmetic and copies ran while one was open for 14% of the time, Pallas kernels for 27%

profile of v1, /device:TPU:25, one launch (start us, length us, event | category | flops | bytes accessed | tf_op | source)
XLA Modules:
  0.0 242.8 jit_solution(11404444773469151185)
XLA Ops:
  1.4 1.3 collective-permute-start.2
  4.4 2.1 collective-permute-start
  6.5 5.6 %fusion.12 = (bf16[1024,1,512]{2,1,0:T(2,128)(2,1)S(1)}, bf16[1024,1,512]{2,1,0:T(2,128)(2,1)S(1)}) fusion(bf16[1024,2,512]{2,1,0:T(2,128)(2,1)} %param.14), kind=kLoop, calls=%fused_computation.58 | loop fusion | bytes 4194304 | tf_op jit(solution)/shard_map/slice | solution.py:403
  12.2 2.0 copy_bitcast_fusion
  14.2 1.3 decays.1
  20.3 11.2 %front0.1 = (bf16[1024,2048]{1,0:T(8,128)(2,1)}, bf16[1024,256]{1,0:T(8,128)(2,1)S(1)}, bf16[1024,256]{1,0:T(8,128)(2,1)S(1)}, f32[256,2048]{1,0:T(8,128)}) custom-call(bf16[1024,4096]{1,0:T(8,128)(2,1)} %feat_ref.3, bf16[16,4096]{1,0:T(8,128)(2,1)S(1)} %pad_slice_fusion.2.halo_ref, bf16[4,4096]{1,0:T(4,128)(2,1)S(1)} %copy-done.15, ...), custom_call_target="tpu_custom_call" | custom-call | flops 8000000000 | bytes 8388608 | tf_op jit(solution)/shard_map/front0/pallas_call | solution.py:169
  31.5 2.0 select_convert_fusion.5
  33.7 11.4 %front1.1 = (bf16[1024,2048]{1,0:T(8,128)(2,1)}, bf16[1024,256]{1,0:T(8,128)(2,1)S(1)}, bf16[1024,256]{1,0:T(8,128)(2,1)S(1)}, f32[256,2048]{1,0:T(8,128)}) custom-call(bf16[1024,4096]{1,0:T(8,128)(2,1)} %feat_ref.3, bf16[16,4096]{1,0:T(8,128)(2,1)S(1)} %pad_slice_fusion.2.halo_ref, bf16[4,4096]{1,0:T(4,128)(2,1)S(1)} %copy-done.15, ...), custom_call_target="tpu_custom_call" | custom-call | flops 8000000000 | bytes 8388608 | tf_op jit(solution)/shard_map/front1/pallas_call | solution.py:169
  45.9 2.6 %select_convert_fusion.2 = bf16[256,1024]{1,0:T(8,128)(2,1)} fusion(f32[256,2048]{1,0:T(8,128)} %get-tuple-element.32, pred[]{:T(512)S(6)} %eq.5), kind=kLoop, calls=%fused_computation.22 | loop fusion | flops 262144 | bytes 1572865 | tf_op jit(solution)/shard_map/convert_element_type | solution.py:360
  48.5 1.3 collective-permute-start.9
  49.8 2.6 %fusion.9 = (bf16[256,1024]{1,0:T(8,128)(2,1)}, f32[256,1024]{1,0:T(8,128)}) fusion(f32[1024]{0:T(1024)S(1)} %bitcast.42, bf16[256,1024]{1,0:T(8,128)(2,1)} %collective-permute-done.1, f32[1024]{0:T(1024)S(1)} %bitcast.36, pred[]{:T(512)S(6)} %eq.5, f32[256,2048]{1,0:T(8,128)S(1)} %copy-done.24), kind=kLoop, calls=%fused_computation.33 | loop fusion | flops 2097152 | bytes 4202497 | tf_op jit(solution)/shard_map/convert_element_type | solution.py:366
  52.4 1.3 collective-permute-start.3
  53.9 1.3 collective-permute-start.4
  55.2 5.8 %collective-permute-done.9 = bf16[256,1024]{1,0:T(8,128)(2,1)} collective-permute-done((bf16[256,1024]{1,0:T(8,128)(2,1)}, bf16[256,1024]{1,0:T(8,128)(2,1)}, u32[]{:S(2)}, u32[]{:S(2)}) %collective-permute-start.9) | collective-permute-done | bytes 524320 | tf_op jit(solution)/shard_map/ppermute | solution.py:353
  61.0 2.1 fusion.8
  63.1 1.3 collective-permute-start.10
  64.4 1.8 collective-permute-done.3
  66.2 1.9 fusion.1
  68.1 1.5 collective-permute-start.5
  72.5 14.6 %spans1.1.y_ref = f32[1024,2048]{1,0:T(8,128)} custom-call(bf16[1024,2048]{1,0:T(8,128)(2,1)} %get-tuple-element.29.xh_ref, bf16[1024,256]{1,0:T(8,128)(2,1)S(1)} %copy-done.21, bf16[1024,256]{1,0:T(8,128)(2,1)S(1)} %get-tuple-element.31.out_ref, f32[1024,128]{1,0:T(8,128)S(1)} %get-tuple-element.23.col_ref, f32[64,1024]{1,0:T(8,128)S(1)} %get-tuple-element.24.row_ref, ...), custom_call_target="tpu_custom_call" | custom-call | flops 8000000000 | bytes 12582912 | tf_op jit(solution)/shard_map/spans1/pallas_call | solution.py:255
  87.1 1.4 fusion.3
  88.5 1.3 collective-permute-start.11
  89.8 22.0 %collective-permute-done.5 = bf16[256,1024]{1,0:T(8,128)(2,1)S(1)} collective-permute-done((bf16[256,1024]{1,0:T(8,128)(2,1)S(1)}, bf16[256,1024]{1,0:T(8,128)(2,1)S(1)}, u32[]{:S(2)}, u32[]{:S(2)}) %collective-permute-start.5) | collective-permute-done | bytes 524320 | tf_op jit(solution)/shard_map/ppermute | solution.py:345
  111.8 1.6 select_convert_fusion.4
  113.4 2.5 %collective-permute-start.6 = (bf16[256,1024]{1,0:T(8,128)(2,1)S(1)}, bf16[256,1024]{1,0:T(8,128)(2,1)S(1)}, u32[]{:S(2)}, u32[]{:S(2)}) collective-permute-start(bf16[256,1024]{1,0:T(8,128)(2,1)S(1)} %select_convert_fusion.4), channel_id=1, source_target_pairs={{0,4},{4,0},{8,12},{12,8},{16,20},{20,16},{24,28},{28,24},{1,5},{5... | collective-permute-start | bytes 1572872 | tf_op jit(solution)/shard_map/ppermute | solution.py:353
  115.9 14.4 %spans0.1.y_ref = f32[1024,2048]{1,0:T(8,128)} custom-call(bf16[1024,2048]{1,0:T(8,128)(2,1)} %get-tuple-element.20.xh_ref, bf16[1024,256]{1,0:T(8,128)(2,1)S(1)} %copy-done.19, bf16[1024,256]{1,0:T(8,128)(2,1)S(1)} %get-tuple-element.22.out_ref, f32[1024,128]{1,0:T(8,128)S(1)} %get-tuple-element.23.col_ref, f32[64,1024]{1,0:T(8,128)S(1)} %get-tuple-element.24.row_ref, ...), custom_call_target="tpu_custom_call" | custom-call | flops 8000000000 | bytes 12582912 | tf_op jit(solution)/shard_map/spans0/pallas_call | solution.py:255
  130.3 1.4 select_convert_fusion.1
  131.8 1.7 broadcast_select_fusion.1
  133.6 3.5 %back0.4 = bf16[256,2048]{1,0:T(8,128)(2,1)} custom-call(s32[1]{0:T(128)} %bitcast.blk_ref, f32[1024,2048]{1,0:T(8,128)} %spans0.1.y_ref, bf16[1024,256]{1,0:T(8,128)(2,1)S(1)} %get-tuple-element.22.out_ref, bf16[1024,128]{1,0:T(8,128)(2,1)S(1)} %get-tuple-element.27.edev_ref, bf16[128,4096]{1,0:T(8,128)(2,1)S(1)} %copy-done, ...), custom_call_target="tpu_custom_call" | custom-call | flops 1000000000 | bytes 5767168 | tf_op jit(solution)/shard_map/back0/pallas_call | solution.py:332
  137.1 6.5 %collective-permute-start.7 = (bf16[256,2048]{1,0:T(8,128)(2,1)}, bf16[256,2048]{1,0:T(8,128)(2,1)}, u32[]{:S(2)}, u32[]{:S(2)}) collective-permute-start(bf16[256,2048]{1,0:T(8,128)(2,1)} %back0.4), channel_id=1, source_target_pairs={{0,3},{1,2},{2,1},{3,0},{4,7},{5,6},{6,5},{7,4},{8,11},{9,10},{10,... | collective-permute-start | bytes 3145736 | tf_op jit(solution)/shard_map/ppermute | solution.py:464
  143.7 3.6 %back0.5 = bf16[256,2048]{1,0:T(8,128)(2,1)} custom-call(s32[1]{0:T(128)} %bitcast.12.blk_ref, f32[1024,2048]{1,0:T(8,128)} %spans0.1.y_ref, bf16[1024,256]{1,0:T(8,128)(2,1)S(1)} %get-tuple-element.22.out_ref, bf16[1024,128]{1,0:T(8,128)(2,1)S(1)} %get-tuple-element.27.edev_ref, bf16[128,4096]{1,0:T(8,128)(2,1)S(1)} %copy-done, ...), custom_call_target="tpu_custom_call" | custom-call | flops 1000000000 | bytes 5767168 | tf_op jit(solution)/shard_map/back0/pallas_call | solution.py:332
  147.5 1.6 broadcast_select_fusion.3
  149.1 3.5 %back1.4 = bf16[256,2048]{1,0:T(8,128)(2,1)} custom-call(s32[1]{0:T(128)} %bitcast.blk_ref, f32[1024,2048]{1,0:T(8,128)} %spans1.1.y_ref, bf16[1024,256]{1,0:T(8,128)(2,1)S(1)} %copy-done.4, bf16[1024,128]{1,0:T(8,128)(2,1)S(1)} %get-tuple-element.27.edev_ref, bf16[128,4096]{1,0:T(8,128)(2,1)S(1)} %copy-done, ...), custom_call_target="tpu_custom_call" | custom-call | flops 1000000000 | bytes 5767168 | tf_op jit(solution)/shard_map/back1/pallas_call | solution.py:332
  154.0 2.8 %back1.5 = bf16[256,2048]{1,0:T(8,128)(2,1)S(1)} custom-call(s32[1]{0:T(128)} %bitcast.12.blk_ref, f32[1024,2048]{1,0:T(8,128)} %spans1.1.y_ref, bf16[1024,256]{1,0:T(8,128)(2,1)S(1)} %copy-done.5, bf16[1024,128]{1,0:T(8,128)(2,1)S(1)} %get-tuple-element.27.edev_ref, bf16[128,4096]{1,0:T(8,128)(2,1)S(1)} %copy-done, ...), custom_call_target="tpu_custom_call" | custom-call | flops 1000000000 | bytes 5767168 | tf_op jit(solution)/shard_map/back1/pallas_call | solution.py:332
  156.8 1.3 collective-permute-start.14
  158.1 2.7 %back0.6 = bf16[256,2048]{1,0:T(8,128)(2,1)S(1)} custom-call(s32[1]{0:T(128)} %bitcast.17.blk_ref, f32[1024,2048]{1,0:T(8,128)} %spans0.1.y_ref, bf16[1024,256]{1,0:T(8,128)(2,1)S(1)} %copy-done.2, bf16[1024,128]{1,0:T(8,128)(2,1)S(1)} %get-tuple-element.27.edev_ref, bf16[128,4096]{1,0:T(8,128)(2,1)S(1)} %copy-done, ...), custom_call_target="tpu_custom_call" | custom-call | flops 1000000000 | bytes 5767168 | tf_op jit(solution)/shard_map/back0/pallas_call | solution.py:332
  161.5 2.7 %back1.6 = bf16[256,2048]{1,0:T(8,128)(2,1)S(1)} custom-call(s32[1]{0:T(128)} %bitcast.17.blk_ref, f32[1024,2048]{1,0:T(8,128)} %spans1.1.y_ref, bf16[1024,256]{1,0:T(8,128)(2,1)S(1)} %copy-done.5, bf16[1024,128]{1,0:T(8,128)(2,1)S(1)} %get-tuple-element.27.edev_ref, bf16[128,4096]{1,0:T(8,128)(2,1)S(1)} %copy-done, ...), custom_call_target="tpu_custom_call" | custom-call | flops 1000000000 | bytes 5767168 | tf_op jit(solution)/shard_map/back1/pallas_call | solution.py:332
  164.2 2.7 %back1.7 = bf16[256,2048]{1,0:T(8,128)(2,1)S(1)} custom-call(s32[1]{0:T(128)} %bitcast.18.blk_ref, f32[1024,2048]{1,0:T(8,128)} %spans1.1.y_ref, bf16[1024,256]{1,0:T(8,128)(2,1)S(1)} %copy-done.5, bf16[1024,128]{1,0:T(8,128)(2,1)S(1)} %get-tuple-element.27.edev_ref, bf16[128,4096]{1,0:T(8,128)(2,1)S(1)} %copy-done, ...), custom_call_target="tpu_custom_call" | custom-call | flops 1000000000 | bytes 5767168 | tf_op jit(solution)/shard_map/back1/pallas_call | solution.py:332
  167.0 2.7 %back0.7 = bf16[256,2048]{1,0:T(8,128)(2,1)S(1)} custom-call(s32[1]{0:T(128)} %bitcast.18.blk_ref, f32[1024,2048]{1,0:T(8,128)} %spans0.1.y_ref, bf16[1024,256]{1,0:T(8,128)(2,1)S(1)} %copy-done.2, bf16[1024,128]{1,0:T(8,128)(2,1)S(1)} %get-tuple-element.27.edev_ref, bf16[128,4096]{1,0:T(8,128)(2,1)S(1)} %copy-done, ...), custom_call_target="tpu_custom_call" | custom-call | flops 1000000000 | bytes 5767168 | tf_op jit(solution)/shard_map/back0/pallas_call | solution.py:332
  170.8 1.3 constant_dynamic-update-slice_fusion.7
  172.2 18.2 %collective-permute-done.8 = bf16[256,2048]{1,0:T(8,128)(2,1)} collective-permute-done((bf16[256,2048]{1,0:T(8,128)(2,1)}, bf16[256,2048]{1,0:T(8,128)(2,1)}, u32[]{:S(2)}, u32[]{:S(2)}) %collective-permute-start.8) | collective-permute-done | bytes 1048608 | tf_op jit(solution)/shard_map/ppermute | solution.py:464
  190.4 1.3 constant_dynamic-update-slice_fusion.6
  191.7 21.1 %collective-permute-done.13 = bf16[256,2048]{1,0:T(8,128)(2,1)} collective-permute-done((bf16[256,2048]{1,0:T(8,128)(2,1)}, bf16[256,2048]{1,0:T(8,128)(2,1)}, u32[]{:S(2)}, u32[]{:S(2)}) %collective-permute-start.13) | collective-permute-done | bytes 1048608 | tf_op jit(solution)/shard_map/ppermute | solution.py:464
  212.8 1.3 constant_dynamic-update-slice_fusion.5
  214.2 21.1 %collective-permute-done.14 = bf16[256,2048]{1,0:T(8,128)(2,1)} collective-permute-done((bf16[256,2048]{1,0:T(8,128)(2,1)S(1)}, bf16[256,2048]{1,0:T(8,128)(2,1)}, u32[]{:S(2)}, u32[]{:S(2)}) %collective-permute-start.14) | collective-permute-done | bytes 1048608 | tf_op jit(solution)/shard_map/ppermute | solution.py:464
  235.3 1.3 constant_dynamic-update-slice_fusion.4
  236.7 1.3 constant_dynamic-update-slice_fusion.3
  238.3 3.4 %copy-done.23 = bf16[256,16384]{1,0:T(8,128)(2,1)} copy-done((bf16[256,16384]{1,0:T(8,128)(2,1)}, bf16[256,16384]{1,0:T(8,128)(2,1)S(1)}, u32[]{:S(2)}) %copy-start.23) | copy-done | bytes 8388632
  (93 shorter events, 16.7 us)
Async XLA Ops:
  0.0 16.9 %copy-start = (bf16[128,4096]{1,0:T(8,128)(2,1)S(1)}, bf16[128,4096]{1,0:T(8,128)(2,1)}, u32[]{:S(2)}) copy-start(bf16[128,4096]{1,0:T(8,128)(2,1)} %constant.48.clone.spread_ref) | copy-start | bytes 3145732
  0.0 14.2 %copy-start.7 = (f32[64,1024]{1,0:T(8,128)S(1)}, f32[64,1024]{1,0:T(8,128)}, u32[]{:S(2)}) copy-start(f32[64,1024]{1,0:T(8,128)} %log_ref.1) | copy-start | bytes 786436
  0.0 12.2 %copy-start.25 = (bf16[4,2,512]{2,1,0:T(2,128)(2,1)S(1)}, bf16[4,2,512]{2,1,0:T(2,128)(2,1)}, u32[]{:S(2)}) copy-start(bf16[4,2,512]{2,1,0:T(2,128)(2,1)} %param.18) | copy-start | bytes 24580
  0.0 14.2 %copy-start.10 = (f32[64,1024]{1,0:T(8,128)S(1)}, f32[64,1024]{1,0:T(8,128)}, u32[]{:S(2)}) copy-start(f32[64,1024]{1,0:T(8,128)} %step_ref.1) | copy-start | bytes 786436
  0.0 16.9 %copy-start.15 = (bf16[4,4096]{1,0:T(4,128)(2,1)S(1)}, bf16[4,4096]{1,0:T(4,128)(2,1)}, u32[]{:S(2)}) copy-start(bf16[4,4096]{1,0:T(4,128)(2,1)} %taps_ref.3) | copy-start | bytes 98308
  1.4 14.8 %collective-permute-start.2 = (f32[1,4096]{1,0:T(1,128)S(1)}, f32[1,4096]{1,0:T(1,128)S(1)}, u32[]{:S(2)}, u32[]{:S(2)}) collective-permute-start(f32[1,4096]{1,0:T(1,128)S(1)} %broadcast_in_dim_reshape.7), channel_id=1, source_target_pairs={{0,4},{4,0},{8,12},{12,8},{16,20},{20,16},{24,28},{28,24},{1,5},{5... | collective-permute-start | bytes 49160 | tf_op jit(solution)/shard_map/ppermute | solution.py:353
  4.4 11.8 %collective-permute-start = (bf16[3,5120]{1,0:T(4,128)(2,1)S(1)}, bf16[3,5120]{1,0:T(4,128)(2,1)S(1)}, u32[]{:S(2)}, u32[]{:S(2)}) collective-permute-start(bf16[3,5120]{1,0:T(4,128)(2,1)S(1)} %pad_maximum_fusion), channel_id=1, source_target_pairs={{0,4},{4,8},{8,12},{12,16},{16,20},{20,24},{24,28},{1,5},{5,9},{9,... | collective-permute-start | bytes 92168 | tf_op jit(solution)/shard_map/ppermute | solution.py:402
  15.5 0.7 copy-start.13
  16.2 0.7 copy-start.11
  16.9 1.2 copy-start.8
  18.1 1.2 copy-start.9
  19.4 0.9 copy-start.16
  31.5 2.0 copy-start.18
  31.5 112.1 %copy-start.1 = (bf16[1024,256]{1,0:T(8,128)(2,1)}, bf16[1024,256]{1,0:T(8,128)(2,1)S(1)}, u32[]{:S(2)}) copy-start(bf16[1024,256]{1,0:T(8,128)(2,1)S(1)} %get-tuple-element.22.out_ref) | copy-start | bytes 1572868
  33.6 16.2 %copy-start.24 = (f32[256,2048]{1,0:T(8,128)S(1)}, f32[256,2048]{1,0:T(8,128)}, u32[]{:S(2)}) copy-start(f32[256,2048]{1,0:T(8,128)} %get-tuple-element.28) | copy-start | bytes 6291460
  33.6 20.1 %copy-start.26 = (f32[64]{0:T(128)S(1)}, f32[64]{0:T(128)}, u32[]{:S(2)}) copy-start(f32[64]{0:T(128)} %param.19) | copy-start | bytes 772
  33.6 16.2 %collective-permute-start.1 = (bf16[256,1024]{1,0:T(8,128)(2,1)S(1)}, bf16[256,1024]{1,0:T(8,128)(2,1)}, u32[]{:S(2)}, u32[]{:S(2)}) collective-permute-start(bf16[256,1024]{1,0:T(8,128)(2,1)S(1)} %select_convert_fusion.5), channel_id=1, source_target_pairs={{0,4},{4,0},{8,12},{12,8},{16,20},{20,16},{24,28},{28,24},{1,5},{5... | collective-permute-start | bytes 1572872 | tf_op jit(solution)/shard_map/ppermute | solution.py:353
  45.1 0.8 copy-start.20
  45.9 41.2 %copy-start.3 = (bf16[1024,256]{1,0:T(8,128)(2,1)}, bf16[1024,256]{1,0:T(8,128)(2,1)S(1)}, u32[]{:S(2)}) copy-start(bf16[1024,256]{1,0:T(8,128)(2,1)S(1)} %get-tuple-element.31.out_ref) | copy-start | bytes 1572868
  45.9 23.7 %copy-start.17 = (bf16[2,128]{1,0:T(2,128)(2,1)S(1)}, bf16[2,128]{1,0:T(2,128)(2,1)}, u32[]{:S(2)}) copy-start(bf16[2,128]{1,0:T(2,128)(2,1)} %constant.50.clone.halves_ref) | copy-start | bytes 1540
  48.5 12.5 %collective-permute-start.9 = (bf16[256,1024]{1,0:T(8,128)(2,1)}, bf16[256,1024]{1,0:T(8,128)(2,1)}, u32[]{:S(2)}, u32[]{:S(2)}) collective-permute-start(bf16[256,1024]{1,0:T(8,128)(2,1)} %select_convert_fusion.2), channel_id=1, source_target_pairs={{0,4},{4,0},{8,12},{12,8},{16,20},{20,16},{24,28},{28,24},{1,5},{5... | collective-permute-start | bytes 1572872 | tf_op jit(solution)/shard_map/ppermute | solution.py:353
  52.4 13.8 %collective-permute-start.3 = (bf16[256,1024]{1,0:T(8,128)(2,1)}, bf16[256,1024]{1,0:T(8,128)(2,1)}, u32[]{:S(2)}, u32[]{:S(2)}) collective-permute-start(bf16[256,1024]{1,0:T(8,128)(2,1)} %get-tuple-element.45), channel_id=1, source_target_pairs={{0,8},{4,12},{8,16},{12,20},{16,24},{20,28},{1,9},{5,13},{9,17},{1... | collective-permute-start | bytes 1572872 | tf_op jit(solution)/shard_map/ppermute | solution.py:345
  53.9 33.2 %collective-permute-start.4 = (f32[1,4096]{1,0:T(1,128)S(1)}, f32[1,4096]{1,0:T(1,128)S(1)}, u32[]{:S(2)}, u32[]{:S(2)}) collective-permute-start(f32[1,4096]{1,0:T(1,128)S(1)} %mul.135), channel_id=1, source_target_pairs={{0,8},{4,12},{8,16},{12,20},{16,24},{20,28},{1,9},{5,13},{9,17},{1... | collective-permute-start | bytes 49160 | tf_op jit(solution)/shard_map/ppermute | solution.py:345
  63.1 24.0 %collective-permute-start.10 = (bf16[256,1024]{1,0:T(8,128)(2,1)S(1)}, bf16[256,1024]{1,0:T(8,128)(2,1)S(1)}, u32[]{:S(2)}, u32[]{:S(2)}) collective-permute-start(bf16[256,1024]{1,0:T(8,128)(2,1)S(1)} %get-tuple-element.38), channel_id=1, source_target_pairs={{0,8},{4,12},{8,16},{12,20},{16,24},{20,28},{1,9},{5,13},{9,17},{1... | collective-permute-start | bytes 1572872 | tf_op jit(solution)/shard_map/ppermute | solution.py:345
  68.1 43.7 %collective-permute-start.5 = (bf16[256,1024]{1,0:T(8,128)(2,1)S(1)}, bf16[256,1024]{1,0:T(8,128)(2,1)S(1)}, u32[]{:S(2)}, u32[]{:S(2)}) collective-permute-start(bf16[256,1024]{1,0:T(8,128)(2,1)S(1)} %fusion.1), channel_id=1, source_target_pairs={{0,16},{4,20},{8,24},{12,28},{1,17},{5,21},{9,25},{13,29},{2,18},{... | collective-permute-start | bytes 1572872 | tf_op jit(solution)/shard_map/ppermute | solution.py:345
  69.5 1.0 copy-start.12
  70.5 0.9 copy-start.14
  71.4 1.0 copy-start.21
  72.5 39.3 %copy-start.22 = (f32[256,1024]{1,0:T(8,128)S(1)}, f32[256,1024]{1,0:T(8,128)}, u32[]{:S(2)}) copy-start(f32[256,1024]{1,0:T(8,128)} %get-tuple-element.46) | copy-start | bytes 3145732
  72.5 43.4 %copy-start.19 = (bf16[1024,256]{1,0:T(8,128)(2,1)S(1)}, bf16[1024,256]{1,0:T(8,128)(2,1)}, u32[]{:S(2)}) copy-start(bf16[1024,256]{1,0:T(8,128)(2,1)} %copy-done.18) | copy-start | bytes 1572868
  88.5 41.8 %collective-permute-start.11 = (bf16[256,1024]{1,0:T(8,128)(2,1)S(1)}, bf16[256,1024]{1,0:T(8,128)(2,1)S(1)}, u32[]{:S(2)}, u32[]{:S(2)}) collective-permute-start(bf16[256,1024]{1,0:T(8,128)(2,1)S(1)} %fusion.3), channel_id=1, source_target_pairs={{0,16},{4,20},{8,24},{12,28},{1,17},{5,21},{9,25},{13,29},{2,18},{... | collective-permute-start | bytes 1572872 | tf_op jit(solution)/shard_map/ppermute | solution.py:345
  113.4 18.4 %collective-permute-start.6 = (bf16[256,1024]{1,0:T(8,128)(2,1)S(1)}, bf16[256,1024]{1,0:T(8,128)(2,1)S(1)}, u32[]{:S(2)}, u32[]{:S(2)}) collective-permute-start(bf16[256,1024]{1,0:T(8,128)(2,1)S(1)} %select_convert_fusion.4), channel_id=1, source_target_pairs={{0,4},{4,0},{8,12},{12,8},{16,20},{20,16},{24,28},{28,24},{1,5},{5... | collective-permute-start | bytes 1572872 | tf_op jit(solution)/shard_map/ppermute | solution.py:353
  130.3 3.3 %copy-start.6 = (f32[4096]{0:T(1024)S(1)}, f32[4096]{0:T(1024)}, u32[]{:S(2)}) copy-start(f32[4096]{0:T(1024)} %param.20) | copy-start | bytes 49156
  131.7 15.8 %collective-permute-start.12 = (bf16[256,1024]{1,0:T(8,128)(2,1)S(1)}, bf16[256,1024]{1,0:T(8,128)(2,1)S(1)}, u32[]{:S(2)}, u32[]{:S(2)}) collective-permute-start(bf16[256,1024]{1,0:T(8,128)(2,1)S(1)} %select_convert_fusion.1), channel_id=1, source_target_pairs={{0,4},{4,0},{8,12},{12,8},{16,20},{20,16},{24,28},{28,24},{1,5},{5... | collective-permute-start | bytes 1572872 | tf_op jit(solution)/shard_map/ppermute | solution.py:353
  137.1 32.6 %collective-permute-start.7 = (bf16[256,2048]{1,0:T(8,128)(2,1)}, bf16[256,2048]{1,0:T(8,128)(2,1)}, u32[]{:S(2)}, u32[]{:S(2)}) collective-permute-start(bf16[256,2048]{1,0:T(8,128)(2,1)} %back0.4), channel_id=1, source_target_pairs={{0,3},{1,2},{2,1},{3,0},{4,7},{5,6},{6,5},{7,4},{8,11},{9,10},{10,... | collective-permute-start | bytes 3145736 | tf_op jit(solution)/shard_map/ppermute | solution.py:464
  143.7 5.5 %copy-start.4 = (bf16[1024,256]{1,0:T(8,128)(2,1)S(1)}, bf16[1024,256]{1,0:T(8,128)(2,1)}, u32[]{:S(2)}) copy-start(bf16[1024,256]{1,0:T(8,128)(2,1)} %copy-done.3) | copy-start | bytes 1572868
  147.2 43.1 %collective-permute-start.8 = (bf16[256,2048]{1,0:T(8,128)(2,1)}, bf16[256,2048]{1,0:T(8,128)(2,1)}, u32[]{:S(2)}, u32[]{:S(2)}) collective-permute-start(bf16[256,2048]{1,0:T(8,128)(2,1)} %back0.5), channel_id=1, source_target_pairs={{0,2},{1,3},{2,0},{3,1},{4,6},{5,7},{6,4},{7,5},{8,10},{9,11},{10,... | collective-permute-start | bytes 3145736 | tf_op jit(solution)/shard_map/ppermute | solution.py:464
  152.7 60.2 %collective-permute-start.13 = (bf16[256,2048]{1,0:T(8,128)(2,1)}, bf16[256,2048]{1,0:T(8,128)(2,1)}, u32[]{:S(2)}, u32[]{:S(2)}) collective-permute-start(bf16[256,2048]{1,0:T(8,128)(2,1)} %back1.4), channel_id=1, source_target_pairs={{0,3},{1,2},{2,1},{3,0},{4,7},{5,6},{6,5},{7,4},{8,11},{9,10},{10,... | collective-permute-start | bytes 3145736 | tf_op jit(solution)/shard_map/ppermute | solution.py:464
  153.0 1.0 copy-start.5
  154.0 4.1 %copy-start.2 = (bf16[1024,256]{1,0:T(8,128)(2,1)S(1)}, bf16[1024,256]{1,0:T(8,128)(2,1)}, u32[]{:S(2)}) copy-start(bf16[1024,256]{1,0:T(8,128)(2,1)} %copy-done.1) | copy-start | bytes 1572868
  156.8 78.5 %collective-permute-start.14 = (bf16[256,2048]{1,0:T(8,128)(2,1)S(1)}, bf16[256,2048]{1,0:T(8,128)(2,1)}, u32[]{:S(2)}, u32[]{:S(2)}) collective-permute-start(bf16[256,2048]{1,0:T(8,128)(2,1)S(1)} %back1.5), channel_id=1, source_target_pairs={{0,2},{1,3},{2,0},{3,1},{4,6},{5,7},{6,4},{7,5},{8,10},{9,11},{10,... | collective-permute-start | bytes 3145736 | tf_op jit(solution)/shard_map/ppermute | solution.py:464
  160.8 75.8 %collective-permute-start.15 = (bf16[256,2048]{1,0:T(8,128)(2,1)S(1)}, bf16[256,2048]{1,0:T(8,128)(2,1)}, u32[]{:S(2)}, u32[]{:S(2)}) collective-permute-start(bf16[256,2048]{1,0:T(8,128)(2,1)S(1)} %back0.6), channel_id=1, source_target_pairs={{0,1},{1,0},{2,3},{3,2},{4,5},{5,4},{6,7},{7,6},{8,9},{9,8},{10,11... | collective-permute-start | bytes 3145736 | tf_op jit(solution)/shard_map/ppermute | solution.py:464
  169.7 68.4 %collective-permute-start.16 = (bf16[256,2048]{1,0:T(8,128)(2,1)S(1)}, bf16[256,2048]{1,0:T(8,128)(2,1)S(1)}, u32[]{:S(2)}, u32[]{:S(2)}) collective-permute-start(bf16[256,2048]{1,0:T(8,128)(2,1)S(1)} %back1.6), channel_id=1, source_target_pairs={{0,1},{1,0},{2,3},{3,2},{4,5},{5,4},{6,7},{7,6},{8,9},{9,8},{10,11... | collective-permute-start | bytes 3145736 | tf_op jit(solution)/shard_map/ppermute | solution.py:464
  238.3 3.4 %copy-start.23 = (bf16[256,16384]{1,0:T(8,128)(2,1)}, bf16[256,16384]{1,0:T(8,128)(2,1)S(1)}, u32[]{:S(2)}) copy-start(bf16[256,16384]{1,0:T(8,128)(2,1)S(1)} %constant_dynamic-update-slice_fusion.1) | copy-start | bytes 25165828
